TPU v7x, 32 devices: a whole 2x2x4 slice. The times are simulated.
32 devices in a mesh: seq: 4 (over y, x), batch: 8 (over z, core).
Axes of the slice: x: 2, y: 2, z: 4, core: 2. Of those that a mesh axis runs over, the one named last changes fastest.
Arguments:
- inputs: bfloat16 [8, 1024, 768], P('batch', 'seq'), may hold values from -6 to 6
- norm_gain: float32 [2, 2, 768], replicated, may hold values from 0.25 to 1.75
- norm_bias: float32 [2, 2, 768], replicated, may hold values from -3 to 3
- w_in: bfloat16 [2, 768, 3072], replicated, may hold values from -0.21875 to 0.21875
- b_in: float32 [2, 3072], replicated, may hold values from -4 to 4
- w_out: bfloat16 [2, 3072, 768], replicated, may hold values from -0.109375 to 0.109375
- b_out: float32 [2, 768], replicated, may hold values from -3 to 3
- cotangent: float32 [8, 1024, 768], P('batch', 'seq'), may hold values from -6 to 6
Outputs:
- outputs: float32 [8, 1024, 768], P('batch', 'seq')
- input_grad: float32 [8, 1024, 768], P('batch', 'seq')
- norm_gain_grad: float32 [2, 2, 768], replicated
- norm_bias_grad: float32 [2, 2, 768], replicated
- w_in_grad: float32 [2, 768, 3072], P(None, None, ('seq', 'batch'))
- b_in_grad: float32 [2, 3072], replicated
- w_out_grad: float32 [2, 3072, 768], P(None, ('seq', 'batch'))
- b_out_grad: float32 [2, 768], replicated
All inputs are finite; a program needn't handle non-finite values.
Results may differ from a plain program's by a relative error of at most 0.01.
Values may be sent and summed in bfloat16 or wider, within the bound.
No kernel may reach another device: no remote copies, remote signals or barrier semaphores. Data moves between devices by JAX's collectives and lax.ppermute only.
A program may use at most 192 MiB of HBM per device.

v0:
```python
import math

import jax
import jax.numpy as jnp
from jax import lax
from jax.sharding import PartitionSpec as P

eps_norm = 1e-05


def dft_rows(first_row, row_count, modulus):
    row_ids = first_row + jnp.arange(row_count, dtype=jnp.int32)
    col_ids = jnp.arange(modulus, dtype=jnp.int32)
    product = row_ids[:, None] * col_ids[None, :] % modulus
    angles = product.astype(jnp.float32) * (2.0 * math.pi / modulus)
    return (jnp.cos(angles).astype(jnp.bfloat16), jnp.sin(angles).astype(jnp.bfloat16))


def layer_norm(values, gain_vec, bias_vec):
    centered = values - jnp.mean(values, axis=-1, keepdims=True)
    inv_std = lax.rsqrt(jnp.mean(centered * centered, axis=-1, keepdims=True) + eps_norm)
    normed = centered * inv_std
    return (normed * gain_vec + bias_vec, normed, inv_std)


def norm_back(upstream, normed, inv_std, gain_vec):
    gain_grad = jnp.sum(upstream * normed, axis=(0, 1))
    bias_grad = jnp.sum(upstream, axis=(0, 1))
    scaled = upstream * gain_vec
    inner = (
        scaled
        - jnp.mean(scaled, axis=-1, keepdims=True)
        - normed * jnp.mean(scaled * normed, axis=-1, keepdims=True)
    )
    return (inv_std * inner, gain_grad, bias_grad)


def body(inputs, norm_gain, norm_bias, w_in, b_in, w_out, b_out, cotangent):
    seq_count = lax.axis_size("seq")
    local_rows = inputs.shape[1]
    width = inputs.shape[2]
    length = local_rows * seq_count
    layers = w_in.shape[0]
    cos_rows, sin_rows = dft_rows(lax.axis_index("seq") * local_rows, local_rows, length)
    cos_hid, sin_hid = dft_rows(0, width, width)
    hid_table = jnp.concatenate([cos_hid, sin_hid], axis=1)
    dft_scale = 1.0 / math.sqrt(length * width)
    state = inputs.astype(jnp.float32)
    stored = []
    for layer_id in range(layers):
        flat_in = state.astype(jnp.bfloat16)
        spectrum = (
            jnp.einsum("bld,dk->blk", flat_in, hid_table, preferred_element_type=jnp.float32)
            * dft_scale
        )
        spec_both = spectrum.astype(jnp.bfloat16)
        piece = lax.all_gather(spec_both, "seq", axis=1, tiled=True)
        running = jnp.einsum(
            "ln,bnd->bld", cos_rows, piece[..., :width], preferred_element_type=jnp.float32
        )
        mixed = running - jnp.einsum(
            "ln,bnd->bld", sin_rows, piece[..., width:], preferred_element_type=jnp.float32
        )
        hidden, normed_mix, inv_mix = layer_norm(
            state + mixed, norm_gain[layer_id, 0], norm_bias[layer_id, 0]
        )
        hidden_low = hidden.astype(jnp.bfloat16)
        pre_act = (
            jnp.einsum(
                "bld,df->blf", hidden_low, w_in[layer_id], preferred_element_type=jnp.float32
            )
            + b_in[layer_id]
        )
        act_low = jax.nn.gelu(pre_act).astype(jnp.bfloat16)
        branch = (
            jnp.einsum("blf,fd->bld", act_low, w_out[layer_id], preferred_element_type=jnp.float32)
            + b_out[layer_id]
        )
        state, normed_ff, inv_ff = layer_norm(
            hidden + branch, norm_gain[layer_id, 1], norm_bias[layer_id, 1]
        )
        stored.append((hidden_low, pre_act, act_low, normed_mix, inv_mix, normed_ff, inv_ff))
    upstream = cotangent
    win_grads = [None] * layers
    bin_grads = [None] * layers
    wout_grads = [None] * layers
    bout_grads = [None] * layers
    gain_grads = [None] * layers
    bias_grads = [None] * layers
    for layer_id in reversed(range(layers)):
        hidden_low, pre_act, act_low, normed_mix, inv_mix, normed_ff, inv_ff = stored[layer_id]
        resid_ff, gain_ff, bias_ff = norm_back(upstream, normed_ff, inv_ff, norm_gain[layer_id, 1])
        branch_grad = resid_ff.astype(jnp.bfloat16)
        wout_grads[layer_id] = jnp.einsum(
            "blf,bld->fd", act_low, branch_grad, preferred_element_type=jnp.float32
        )
        bout_grads[layer_id] = jnp.sum(branch_grad.astype(jnp.float32), axis=(0, 1))
        act_grad = jnp.einsum(
            "bld,fd->blf", branch_grad, w_out[layer_id], preferred_element_type=jnp.float32
        )
        unused, gelu_pull = jax.vjp(jax.nn.gelu, pre_act)
        pre_grad = gelu_pull(act_grad)[0].astype(jnp.bfloat16)
        win_grads[layer_id] = jnp.einsum(
            "bld,blf->df", hidden_low, pre_grad, preferred_element_type=jnp.float32
        )
        bin_grads[layer_id] = jnp.sum(pre_grad.astype(jnp.float32), axis=(0, 1))
        hidden_grad = resid_ff + jnp.einsum(
            "blf,df->bld", pre_grad, w_in[layer_id], preferred_element_type=jnp.float32
        )
        resid_mix, gain_mix, bias_mix = norm_back(
            hidden_grad, normed_mix, inv_mix, norm_gain[layer_id, 0]
        )
        gain_grads[layer_id] = jnp.stack([gain_mix, gain_ff])
        bias_grads[layer_id] = jnp.stack([bias_mix, bias_ff])
        mix_grad = resid_mix.astype(jnp.bfloat16)
        shard_piece = lax.all_gather(mix_grad, "seq", axis=1, tiled=True)
        cos_term = jnp.einsum(
            "ln,bnd->bld", cos_rows, shard_piece, preferred_element_type=jnp.float32
        )
        sin_term = jnp.einsum(
            "ln,bnd->bld", sin_rows, shard_piece, preferred_element_type=jnp.float32
        )
        summed = jnp.concatenate([cos_term, -sin_term], axis=-1)
        spec_grad = summed.astype(jnp.bfloat16)
        upstream = (
            resid_mix
            + jnp.einsum("blk,dk->bld", spec_grad, hid_table, preferred_element_type=jnp.float32)
            * dft_scale
        )
    win_stack = jnp.stack(win_grads)
    wout_stack = jnp.stack(wout_grads)
    bin_total, bout_total, gain_total, bias_total = lax.psum(
        (jnp.stack(bin_grads), jnp.stack(bout_grads), jnp.stack(gain_grads), jnp.stack(bias_grads)),
        ("seq", "batch"),
    )
    win_total, wout_total = (
        lax.psum_scatter(win_stack, ("seq", "batch"), scatter_dimension=2, tiled=True),
        lax.psum_scatter(wout_stack, ("seq", "batch"), scatter_dimension=1, tiled=True),
    )
    return (state, upstream, gain_total, bias_total, win_total, bin_total, wout_total, bout_total)


def solution(mesh):
    return jax.shard_map(
        body,
        mesh=mesh,
        in_specs=(P("batch", "seq", None), P(), P(), P(), P(), P(), P(), P("batch", "seq", None)),
        out_specs=(
            P("batch", "seq", None),
            P("batch", "seq", None),
            P(),
            P(),
            P(None, None, ("seq", "batch")),
            P(),
            P(None, ("seq", "batch"), None),
            P(),
        ),
        check_vma=False,
    )
```

profile of v0, /device:TPU:0, one launch (start us, length us, event | category | flops | bytes accessed | tf_op | source)
XLA Modules:
  0.0 774.5 jit_solution(8359933497993001509)
XLA Ops:
  7.2 9.9 %sine_convert_fusion = (bf16[768,768]{1,0:T(8,128)(2,1)S(1)}, bf16[768,768]{1,0:T(8,128)(2,1)S(1)}) fusion(), kind=kLoop, calls=%fused_computation.63 | loop fusion | flops 6488064 | bytes 2359296 | tf_op jit(solution)/shard_map/convert_element_type | solution.py:16
  18.2 2.8 fusion.50
  23.2 44.5 %all-gather.11.cloned.1.call-done = bf16[1024,1536]{0,1:T(8,128)(2,1)} async-done(((bf16[256,1536]{0,1:T(8,128)(2,1)}), bf16[1024,1536]{0,1:T(8,128)(2,1)}) %all-gather.11.cloned.1.call-update) | async-done | bytes 3145744 | tf_op jit(solution)/shard_map/all_gather | solution.py:57
  67.7 5.9 fusion.58
  73.7 4.4 fusion.211
  78.3 4.0 fusion.24
  82.4 2.8 fusion.212
  86.1 1.8 fusion.49
  88.2 43.8 %all-gather.13.cloned.1.call-done = bf16[1024,1536]{1,0:T(8,128)(2,1)} async-done(((bf16[256,1536]{1,0:T(8,128)(2,1)}), bf16[1024,1536]{1,0:T(8,128)(2,1)}) %all-gather.13.cloned.1.call-update) | async-done | bytes 3145744 | tf_op jit(solution)/shard_map/all_gather | solution.py:57
  132.1 5.9 fusion.56
  138.1 4.4 fusion.213
  142.8 4.0 fusion.27
  146.8 2.7 fusion.214
  151.3 3.2 convert_reduce_fusion
  154.6 1.7 multiply_reduce_fusion.1
  157.3 30.9 %all-gather.7.cloned.1.call-done = bf16[1,1024,768]{1,2,0:T(8,128)(2,1)} async-done(((bf16[1,256,768]{1,2,0:T(8,128)(2,1)}), bf16[1,1024,768]{1,2,0:T(8,128)(2,1)}) %all-gather.7.cloned.1.call-update) | async-done | bytes 1572880 | tf_op jit(solution)/shard_map/all_gather | solution.py:116
  188.3 5.9 fusion.132
  194.2 5.2 fusion.129
  201.4 5.6 convert_reduce_fusion.1
  207.1 1.7 multiply_reduce_fusion.3
  210.8 3.0 convolution_bitcast_fusion.2
  213.7 1.5 convolution_bitcast_fusion.3
  215.2 7.2 pad_maximum_fusion
  222.4 28.2 %copy.37 = f32[2,768,3072]{1,0,2:T(2,128)} copy(f32[2,768,3072]{2,1,0:T(8,128)} %pad_maximum_fusion) | data formatting | bytes 37748736 | tf_op jit(solution)/shard_map/stack | solution.py:130
  250.9 4.3 convolution_bitcast_fusion
  255.2 2.2 convolution_bitcast_fusion.1
  257.5 6.7 pad_maximum_fusion.1
  266.9 42.4 %all-reduce.1 = (f32[2,2,768]{2,1,0:T(2,128)}, f32[2,2,768]{2,1,0:T(2,128)}, f32[2,3072]{1,0:T(2,128)}, f32[2,768]{1,0:T(2,128)}) all-reduce(f32[2,2,768]{2,1,0:T(2,128)S(1)} %pad_maximum_fusion.4, f32[2,2,768]{2,1,0:T(2,128)S(1)} %pad_maximum_fusion.5, ...), channel_id=1, replica_groups=mesh['seq'=4,'batch'=8] {'seq','batch'}, use_global_device_ids=true, to_apply=%region_20.21 | all-reduce | flops 13824 | bytes 110592 | tf_op jit(solution)/shard_map/psum | solution.py:132
  309.3 5.9 fusion.126
  315.3 5.0 fusion.135
  322.3 233.0 %all-reduce.4.cloned.1.call-done = f32[2,768,3072]{1,0,2:T(2,128)} async-done(((f32[2,768,3072]{1,0,2:T(2,128)}), f32[2,768,3072]{1,0,2:T(2,128)}) %all-reduce.4.cloned.1.call-update) | async-done | bytes 18874384
  557.3 209.9 %reduce-scatter.2.cloned.1.call-done = f32[2,96,768]{2,1,0:T(8,128)} async-done(((f32[2,3072,768]{2,1,0:T(8,128)}), f32[2,96,768]{2,1,0:T(8,128)}) %reduce-scatter.2.cloned.1.call-update) | async-done | bytes 589840 | tf_op jit(solution)/shard_map/reduce_scatter | solution.py:138
  (193 shorter events, 18.3 us)
Async XLA Ops:
  7.2 60.5 %all-gather.11.cloned.1.call-start = ((), (), s32[]{:S(2)}) async-start(), calls=%async_computation.4 | async-start | bytes 3932160 | tf_op jit(solution)/shard_map/all_gather | solution.py:57
  17.1 68.3 %copy-start.12 = (bf16[768,768]{1,0:T(8,128)(2,1)}, bf16[768,768]{1,0:T(8,128)(2,1)S(1)}, u32[]{:S(2)}) copy-start(bf16[768,768]{1,0:T(8,128)(2,1)S(1)} %get-tuple-element.75) | copy-start | bytes 3538948
  21.0 111.1 %all-gather.13.cloned.1.call-start = ((), (), s32[]{:S(2)}) async-start(), calls=%async_computation.5 | async-start | bytes 3932160 | tf_op jit(solution)/shard_map/all_gather | solution.py:57
  21.3 52.4 %copy-start.46 = (s32[256]{0:T(256)}, s32[256]{0:T(256)S(1)}, u32[]{:S(2)}) copy-start(s32[256]{0:T(256)S(1)} %iota_add_fusion) | copy-start | bytes 3076
  67.7 6.0 copy-start.42
  73.7 8.6 %slice-start = ((s8[9437184]{0:T(1024)(128)(4,1)}), s8[4194304]{0:T(1024)(128)(4,1)S(1)}, s32[]{:S(2)}) async-start(s8[9437184]{0:T(1024)(128)(4,1)} %bitcast.238), calls=%async_computation.7 | async-start | bytes 8388608
  73.7 8.6 %slice-start.1 = ((s8[9437184]{0:T(1024)(128)(4,1)}), s8[4194304]{0:T(1024)(128)(4,1)S(1)}, s32[]{:S(2)}) async-start(s8[9437184]{0:T(1024)(128)(4,1)} %bitcast.238), calls=%async_computation.8 | async-start | bytes 8388608
  85.2 52.8 %copy-start.7 = (f32[1,256,768]{1,2,0:T(8,128)}, f32[1,256,768]{1,2,0:T(8,128)S(1)}, u32[]{:S(2)}) copy-start(f32[1,256,768]{1,2,0:T(8,128)S(1)} %get-tuple-element.63) | copy-start | bytes 2359300
  87.9 100.3 %all-gather.7.cloned.1.call-start = ((), (), s32[]{:S(2)}) async-start(), calls=%async_computation.1 | async-start | bytes 1966080 | tf_op jit(solution)/shard_map/all_gather | solution.py:116
  132.1 6.0 copy-start.27
  132.1 6.0 copy-start.35
  132.1 6.0 copy-start.38
  132.1 6.0 copy-start.40
  132.1 6.0 copy-start.43
  132.1 6.0 copy-start.47
  138.1 8.7 %slice-start.3 = ((s8[9437184]{0:T(1024)(128)(4,1)}), s8[4194304]{0:T(1024)(128)(4,1)S(1)}, s32[]{:S(2)}) async-start(s8[9437184]{0:T(1024)(128)(4,1)} %bitcast.240), calls=%async_computation.10 | async-start | bytes 8388608
  138.1 8.7 %slice-start.4 = ((s8[9437184]{0:T(1024)(128)(4,1)}), s8[4194304]{0:T(1024)(128)(4,1)S(1)}, s32[]{:S(2)}) async-start(s8[9437184]{0:T(1024)(128)(4,1)} %bitcast.240), calls=%async_computation.11 | async-start | bytes 8388608
  157.3 152.0 %all-gather.9.cloned.1.call-start = ((), (), s32[]{:S(2)}) async-start(), calls=%async_computation.2 | async-start | bytes 1966080 | tf_op jit(solution)/shard_map/all_gather | solution.py:116
  188.3 5.9 copy-start.45
  194.2 5.3 copy-start.8
  194.2 5.3 copy-start.13
  194.2 5.3 copy-start.17
  200.7 6.4 slice-start.9
  201.4 5.7 copy-start.24
  201.4 5.7 copy-start.30
  201.4 5.7 slice-start.10
  201.4 5.7 slice-start.11
  210.7 344.6 %all-reduce.4.cloned.1.call-start = ((), (), s32[]{:S(2)}) async-start(), calls=%async_computation.6 | async-start | bytes 37748736
  250.6 516.6 %reduce-scatter.2.cloned.1.call-start = ((), (), s32[]{:S(2)}) async-start(), calls=%async_computation.3 | async-start | bytes 19464192 | tf_op jit(solution)/shard_map/reduce_scatter | solution.py:138
  309.3 5.9 copy-start.44
  315.2 5.1 copy-start.14
  315.2 5.1 copy-start.18
  (34 other events, 103.8 us)
Sparse Core Ops, SparseCore 0:
  21.1 46.5 all-gather.10
  88.0 43.9 all-gather.12
  157.4 30.8 all-gather.6
  210.8 30.8 all-gather.8
  250.7 304.5 all-reduce.3
  562.2 205.0 reduce-scatter.1
where the time goes:
time: 785 us; the launch traced here: 774 us
  waiting for transfers between devices  562 us (72%)
  matrix products  85.9 us (11%)
  blocking collectives  42.4 us (5%)
  local copies, waits for them, and re-layouts  39.3 us (5%)
  other arithmetic  28.5 us (4%)
  between operations  15.6 us (2%)
    unnamed x7, waiting for transfers between devices  233 us
    reduce_scatter x1, waiting for transfers between devices, body(): lax.psum_scatter(wout_stack, ('seq', 'batch'), scatter_dimension=1, tiled...  210 us
    all_gather x2, waiting for transfers between devices, body(): piece = lax.all_gather(spec_both, 'seq', axis=1, tiled=True)  88.3 us
    psum x1, blocking collectives, body(): lax.psum((jnp.stack(bin_grads), jnp.stack(bout_grads), jnp.stack(gain_gra...  42.4 us
    all_gather x2, waiting for transfers between devices, body(): shard_piece = lax.all_gather(mix_grad, 'seq', axis=1, tiled=True)  30.9 us
    another operation x1, local copies, waits for them, and re-layouts, body(): win_stack = jnp.stack(win_grads)  28.2 us
  transfers between devices with their start and end apart: 6, of which 5 were waited for; matrix products, arithmetic and copies ran while one was open for 9% of the time, Pallas kernels for 0%

commit v1 on v0

v1 whole, which is shorter than its diff:
```python
import math

import jax
import jax.numpy as jnp
import numpy as np
from jax import lax
from jax.sharding import PartitionSpec as P

eps_norm = 1e-05
bf16 = jnp.bfloat16
f32 = jnp.float32


def np_tables(modulus):
    ids = np.arange(modulus, dtype=np.int64)
    product = (ids[:, None] * ids[None, :]) % modulus
    angles = product.astype(np.float32) * np.float32(2.0 * math.pi / modulus)
    return np.cos(angles).astype(bf16), np.sin(angles).astype(bf16)


def seq_tables(length, seq_count):
    rows = length // seq_count
    cos_t, sin_t = np_tables(length)
    out = np.zeros((seq_count, 2 * rows, length), dtype=bf16)
    for s in range(seq_count):
        own = slice(s * rows, (s + 1) * rows)
        for m in range(seq_count):
            src = slice((s ^ m) * rows, ((s ^ m) + 1) * rows)
            dst = slice(m * rows, (m + 1) * rows)
            out[s, :rows, dst] = cos_t[own, src]
            out[s, rows:, dst] = sin_t[own, src]
    return out


def xor_send(value, axis, mask):
    size = lax.axis_size(axis)
    return lax.ppermute(value, axis, [(i, i ^ mask) for i in range(size)])


def gather_blocks(block):
    return [block] + [xor_send(block, "seq", m) for m in range(1, lax.axis_size("seq"))]


def layer_norm(values, gain_vec, bias_vec):
    centered = values - jnp.mean(values, axis=-1, keepdims=True)
    inv_std = lax.rsqrt(jnp.mean(centered * centered, axis=-1, keepdims=True) + eps_norm)
    normed = centered * inv_std
    return (normed * gain_vec + bias_vec, normed, inv_std)


def norm_back(upstream, normed, inv_std, gain_vec):
    gain_grad = jnp.sum(upstream * normed, axis=0)
    bias_grad = jnp.sum(upstream, axis=0)
    scaled = upstream * gain_vec
    inner = (
        scaled
        - jnp.mean(scaled, axis=-1, keepdims=True)
        - normed * jnp.mean(scaled * normed, axis=-1, keepdims=True)
    )
    return (inv_std * inner, gain_grad, bias_grad)


def gelu_both(z):
    k = math.sqrt(2.0 / math.pi)
    z2 = z * z
    t = jnp.tanh(k * z * (1.0 + 0.044715 * z2))
    half = 0.5 * (1.0 + t)
    slope = half + 0.5 * z * (1.0 - t * t) * (k * (1.0 + 3 * 0.044715 * z2))
    return z * half, slope


def dot(a, b, dims=((1,), (0,))):
    return lax.dot_general(a, b, (dims, ((), ())), preferred_element_type=f32)


def exchange_sum(part, axis_name, bit, dim, out_dtype):
    mine = (lax.axis_index(axis_name) >> bit) & 1
    keep = lax.dynamic_index_in_dim(part, mine, dim, keepdims=False)
    give = lax.dynamic_index_in_dim(part, 1 - mine, dim, keepdims=False)
    got = xor_send(give, axis_name, 1 << bit)
    return (keep.astype(f32) + got.astype(f32)).astype(out_dtype)


def scatter_sum(grad, flip):
    seq_bits = lax.axis_size("seq").bit_length() - 1
    batch_bits = lax.axis_size("batch").bit_length() - 1
    slots = seq_bits + batch_bits
    part = grad.reshape((2,) * slots + (-1, grad.shape[-1]))
    order = [("batch", 0)]
    seq_order = list(range(seq_bits))
    if flip:
        seq_order.reverse()
    order += [("seq", b) for b in seq_order]
    order += [("batch", b) for b in range(1, batch_bits)]
    dims = [("seq", b) for b in reversed(range(seq_bits))] + [("batch", b) for b in reversed(range(batch_bits))]
    for n, (axis_name, bit) in enumerate(order):
        dim = dims.index((axis_name, bit))
        dims.pop(dim)
        part = exchange_sum(part, axis_name, bit, dim, f32 if n == slots - 1 else bf16)
    return part


def all_sum(vec):
    for axis_name in ("batch", "seq"):
        for bit in range(lax.axis_size(axis_name).bit_length() - 1):
            vec = vec + xor_send(vec, axis_name, 1 << bit)
    return vec


def body(tables, hid_tables, inputs, norm_gain, norm_bias, w_in, b_in, w_out, b_out, cotangent):
    seq_count = lax.axis_size("seq")
    rows = inputs.shape[1]
    width = inputs.shape[2]
    length = rows * seq_count
    layers = w_in.shape[0]
    table = lax.dynamic_index_in_dim(jnp.asarray(tables), lax.axis_index("seq"), 0, keepdims=False)
    cos_hid, sin_hid = (jnp.asarray(t) for t in hid_tables)
    dft_scale = 1.0 / math.sqrt(length * width)

    def mix(block):
        pieces = jnp.concatenate(gather_blocks(block), axis=0)
        spec = (dot(table, pieces) * dft_scale).astype(bf16)
        return dot(spec[:rows], cos_hid) - dot(spec[rows:], sin_hid)

    state = inputs[0].astype(f32)
    stored = []
    for layer_id in range(layers):
        mixed = mix(state.astype(bf16))
        hidden, normed_mix, inv_mix = layer_norm(state + mixed, norm_gain[layer_id, 0], norm_bias[layer_id, 0])
        hidden_low = hidden.astype(bf16)
        act, slope = gelu_both(dot(hidden_low, w_in[layer_id]) + b_in[layer_id])
        act_low, slope = act.astype(bf16), slope.astype(bf16)
        branch = dot(act_low, w_out[layer_id]) + b_out[layer_id]
        state, normed_ff, inv_ff = layer_norm(hidden + branch, norm_gain[layer_id, 1], norm_bias[layer_id, 1])
        stored.append((hidden_low, slope, act_low, normed_mix, inv_mix, normed_ff, inv_ff))
    upstream = cotangent[0]
    win_out, wout_out, small_out = [None] * layers, [None] * layers, [None] * layers
    for layer_id in reversed(range(layers)):
        hidden_low, slope, act_low, normed_mix, inv_mix, normed_ff, inv_ff = stored[layer_id]
        resid_ff, gain_ff, bias_ff = norm_back(upstream, normed_ff, inv_ff, norm_gain[layer_id, 1])
        branch_grad = resid_ff.astype(bf16)
        bout = jnp.sum(branch_grad.astype(f32), axis=0)
        wout = dot(act_low, branch_grad, ((0,), (0,))).astype(bf16)
        pre_grad = (dot(branch_grad, w_out[layer_id], ((1,), (1,))) * slope.astype(f32)).astype(bf16)
        win = dot(pre_grad, hidden_low, ((0,), (0,))).astype(bf16)
        bin_ = jnp.sum(pre_grad.astype(f32), axis=0)
        hidden_grad = resid_ff + dot(pre_grad, w_in[layer_id], ((1,), (1,)))
        resid_mix, gain_mix, bias_mix = norm_back(hidden_grad, normed_mix, inv_mix, norm_gain[layer_id, 0])
        wout_out[layer_id] = scatter_sum(wout, False)
        win_out[layer_id] = scatter_sum(win, True).T
        small_out[layer_id] = all_sum(jnp.concatenate([gain_mix, gain_ff, bias_mix, bias_ff, bout, bin_]))
        upstream = resid_mix + mix(resid_mix.astype(bf16))
    small = jnp.stack(small_out)
    gains = small[:, : 2 * width].reshape(layers, 2, width)
    biases = small[:, 2 * width : 4 * width].reshape(layers, 2, width)
    bout = small[:, 4 * width : 5 * width]
    bin_ = small[:, 5 * width :]
    return (state[None], upstream[None], gains, biases, jnp.stack(win_out), bin_, jnp.stack(wout_out), bout)


def solution(mesh):
    def run(inputs, norm_gain, norm_bias, w_in, b_in, w_out, b_out, cotangent):
        tables = seq_tables(inputs.shape[1], mesh.shape["seq"])
        hid_tables = np_tables(inputs.shape[2])

        def inner(*args):
            return body(tables, hid_tables, *args)

        return jax.shard_map(
            inner,
            mesh=mesh,
            in_specs=(P("batch", "seq", None), P(), P(), P(), P(), P(), P(), P("batch", "seq", None)),
            out_specs=(
                P("batch", "seq", None),
                P("batch", "seq", None),
                P(),
                P(),
                P(None, None, ("seq", "batch")),
                P(),
                P(None, ("seq", "batch"), None),
                P(),
            ),
            check_vma=False,
        )(inputs, norm_gain, norm_bias, w_in, b_in, w_out, b_out, cotangent)

    return run
```

time: 785 us -> 287 us (0.37)
  waiting for transfers between devices: 562 us -> 140 us
  starting transfers between devices: 0.5 us -> 43.7 us
  blocking collectives: 42.4 us -> 0 us
  matrix products: 85.9 us -> 55 us
  local copies, waits for them, and re-layouts: 39.3 us -> 22.7 us
  between operations: 15.6 us -> 1.96 us
  other arithmetic: 28.5 us -> 19.6 us
    unnamed x7 -> x0, waiting for transfers between devices: 233 us -> none
    reduce_scatter x1 -> x0, waiting for transfers between devices: 210 us -> none  [body(): lax.psum_scatter(wout_stack, ('seq', 'batch'), scatter_dimension=1, tiled...]
    ppermute x0 -> x42, waiting for transfers between devices: none -> 140 us  [xor_send(): return lax.ppermute(value, axis, [(i, i ^ mask) for i in range(size)])]
    all_gather x4 -> x0, waiting for transfers between devices: 119 us -> none  [the longest x2 88.3 us: body(): piece = lax.all_gather(spec_both, 'seq', axis=1, tiled=True)]
    ppermute x0 -> x42, starting transfers between devices: none -> 43.7 us  [xor_send(): return lax.ppermute(value, axis, [(i, i ^ mask) for i in range(size)])]
    psum x1 -> x0, blocking collectives: 42.4 us -> none  [body(): lax.psum((jnp.stack(bin_grads), jnp.stack(bout_grads), jnp.stack(gain_gra...]
    dot_general x24, matrix products: 85.9 us -> 55 us  [dot(): return lax.dot_general(a, b, (dims, ((), ())), preferred_element_type=f32)]
    another operation x11 -> x2, local copies, waits for them, and re-layouts: 28.3 us -> 0.04 us  [body(): small = jnp.stack(small_out)]
  transfers between devices with their start and end apart: 6 -> 42, of which waited for: 5 -> 24; matrix products, arithmetic and copies ran while one was open for 9% -> 24% of each run, Pallas kernels for 0% -> 0%
where the time goes in v1:
time: 287 us; the launch traced here: 283 us
  waiting for transfers between devices  140 us (49%)
  matrix products  55 us (19%)
  starting transfers between devices  43.7 us (15%)
  local copies, waits for them, and re-layouts  22.7 us (8%)
  other arithmetic  19.6 us (7%)
    ppermute x42, waiting for transfers between devices, xor_send(): return lax.ppermute(value, axis, [(i, i ^ mask) for i in range(size)])  140 us
    dot_general x24, matrix products, dot(): return lax.dot_general(a, b, (dims, ((), ())), preferred_element_type=f32)  55 us
    ppermute x42, starting transfers between devices, xor_send(): return lax.ppermute(value, axis, [(i, i ^ mask) for i in range(size)])  43.7 us
    convert_element_type x16, other arithmetic, exchange_sum(): return (keep.astype(f32) + got.astype(f32)).astype(out_dtype)  10.3 us
    dynamic_slice x4, local copies, waits for them, and re-layouts, exchange_sum(): keep = lax.dynamic_index_in_dim(part, mine, dim, keepdims=False)  6.89 us
    dynamic_slice x4, local copies, waits for them, and re-layouts, exchange_sum(): give = lax.dynamic_index_in_dim(part, 1 - mine, dim, keepdims=False)  6.38 us
  transfers between devices with their start and end apart: 42, of which 24 were waited for; matrix products, arithmetic and copies ran while one was open for 24% of the time, Pallas kernels for 0%

profile of v1, /device:TPU:0, one launch (start us, length us, event | category | flops | bytes accessed | tf_op | source)
XLA Modules:
  0.0 283.4 jit_solution(14978116270887288730)
XLA Ops:
  0.6 3.0 %collective-permute-start = (bf16[256,768]{1,0:T(8,128)(2,1)}, bf16[256,768]{1,0:T(8,128)(2,1)S(1)}, u32[]{:S(2)}, u32[]{:S(2)}) collective-permute-start(bf16[256,768]{1,0:T(8,128)(2,1)} %bitcast.230), channel_id=1, source_target_pairs={{0,8},{8,0},{16,24},{24,16},{1,9},{9,1},{17,25},{25,17},{2,10},{10... | collective-permute-start | bytes 1179656 | tf_op jit(solution)/shard_map/ppermute | solution.py:37
  9.5 4.3 %collective-permute-done = bf16[256,768]{1,0:T(8,128)(2,1)S(1)} collective-permute-done((bf16[256,768]{1,0:T(8,128)(2,1)}, bf16[256,768]{1,0:T(8,128)(2,1)S(1)}, u32[]{:S(2)}, u32[]{:S(2)}) %collective-permute-start) | collective-permute-done | bytes 393248 | tf_op jit(solution)/shard_map/ppermute | solution.py:37
  13.8 9.1 %collective-permute-done.1 = bf16[256,768]{1,0:T(8,128)(2,1)S(1)} collective-permute-done((bf16[256,768]{1,0:T(8,128)(2,1)}, bf16[256,768]{1,0:T(8,128)(2,1)S(1)}, u32[]{:S(2)}, u32[]{:S(2)}) %collective-permute-start.1) | collective-permute-done | bytes 393248 | tf_op jit(solution)/shard_map/ppermute | solution.py:37
  22.9 2.3 multiply_convert_fusion.5
  27.3 4.0 %fusion.28 = f32[256,3072]{1,0:T(8,128)S(1)} fusion(bf16[2,768,3072]{2,1,0:T(8,128)(2,1)} %param.14, f32[3072]{0:T(1024)S(1)} %bitcast.235, f32[256,768]{1,0:T(8,128)S(1)} %get-tuple-element.55, f32[768]{0:T(1024)S(1)} %get-tuple-element.29, f32[768]{0:T(1024)S(1)} %get-tuple-element.70, f32[256]{0:T(256)S(1)} %add_rsqrt_fusion.3, ...), kind=kOutput, calls=%fused_computation.36 | convolution fusion | flops 1209729024 | bytes 8671232 | tf_op jit(solution)/shard_map/dot_general | solution.py:73
  40.6 6.9 %collective-permute-done.3 = bf16[256,768]{1,0:T(8,128)(2,1)} collective-permute-done((bf16[256,768]{1,0:T(8,128)(2,1)S(1)}, bf16[256,768]{1,0:T(8,128)(2,1)}, u32[]{:S(2)}, u32[]{:S(2)}) %collective-permute-start.3) | collective-permute-done | bytes 393248 | tf_op jit(solution)/shard_map/ppermute | solution.py:37
  47.5 7.3 %collective-permute-done.4 = bf16[256,768]{1,0:T(8,128)(2,1)} collective-permute-done((bf16[256,768]{1,0:T(8,128)(2,1)S(1)}, bf16[256,768]{1,0:T(8,128)(2,1)}, u32[]{:S(2)}, u32[]{:S(2)}) %collective-permute-start.4) | collective-permute-done | bytes 393248 | tf_op jit(solution)/shard_map/ppermute | solution.py:37
  54.8 2.7 multiply_convert_fusion.4
  59.0 3.9 %fusion.34 = f32[256,3072]{1,0:T(8,128)S(1)} fusion(bf16[2,768,3072]{2,1,0:T(8,128)(2,1)} %param.14, f32[3072]{0:T(1024)S(1)} %bitcast.234, f32[256,768]{1,0:T(8,128)S(1)} %get-tuple-element.59, f32[768]{0:T(1024)S(1)} %copy-done.20, f32[768]{0:T(1024)S(1)} %get-tuple-element.69, f32[256]{0:T(256)S(1)} %add_rsqrt_fusion.1, f32[256]{0:T(256)S(1)} %broadcast_multiply_fusion.9), kind=kOutput, calls=%fused_computation.38 | convolution fusion | flops 1209729024 | bytes 8671232 | tf_op jit(solution)/shard_map/dot_general | solution.py:73
  67.0 3.0 %convert_reduce_fusion = (f32[3072]{0:T(1024)S(1)}, bf16[256,3072]{1,0:T(8,128)(2,1)S(1)}) fusion(f32[256,3072]{1,0:T(8,128)S(1)} %fusion.34, bf16[2,3072,768]{2,1,0:T(8,128)(2,1)S(1)} %bitcast.237, f32[256,768]{1,0:T(8,128)S(1)} %get-tuple-element.36), kind=kOutput, calls=%fused_computation.42 | convolution fusion | flops 1225454592 | bytes 10235904 | tf_op jit(solution)/shard_map/dot_general | solution.py:73
  79.8 2.6 collective-permute-start.19
  88.4 4.4 %collective-permute-done.20 = f32[6912]{0:T(1024)S(1)} collective-permute-done((f32[6912]{0:T(1024)S(1)}, f32[6912]{0:T(1024)S(1)}, u32[]{:S(2)}, u32[]{:S(2)}) %collective-permute-start.20) | collective-permute-done | bytes 27680 | tf_op jit(solution)/shard_map/ppermute | solution.py:37
  101.5 2.3 convolution_convert_fusion.1
  103.8 13.7 %convert_reduce_fusion.1 = (f32[3072]{0:T(1024)S(1)}, bf16[256,3072]{1,0:T(8,128)(2,1)S(1)}) fusion(f32[256,3072]{1,0:T(8,128)S(1)} %copy-done.31, bf16[2,3072,768]{2,1,0:T(8,128)(2,1)S(1)} %bitcast.237, f32[256,768]{1,0:T(8,128)S(1)} %get-tuple-element.34), kind=kOutput, calls=%fused_computation.43 | convolution fusion | flops 1225454592 | bytes 10235904 | tf_op jit(solution)/shard_map/dot_general | solution.py:73
  124.1 2.3 collective-permute-done.13
  126.4 2.6 collective-permute-start.14
  135.3 6.7 %collective-permute-done.15 = f32[6912]{0:T(1024)S(1)} collective-permute-done((f32[6912]{0:T(1024)S(1)}, f32[6912]{0:T(1024)S(1)}, u32[]{:S(2)}, u32[]{:S(2)}) %collective-permute-start.15) | collective-permute-done | bytes 27680 | tf_op jit(solution)/shard_map/ppermute | solution.py:37
  153.2 9.1 %collective-permute-done.9 = bf16[256,768]{1,0:T(8,128)(2,1)S(1)} collective-permute-done((bf16[256,768]{1,0:T(8,128)(2,1)}, bf16[256,768]{1,0:T(8,128)(2,1)S(1)}, u32[]{:S(2)}, u32[]{:S(2)}) %collective-permute-start.9) | collective-permute-done | bytes 393248 | tf_op jit(solution)/shard_map/ppermute | solution.py:37
  162.2 2.5 multiply_convert_fusion.2
  166.7 2.5 fusion
  170.5 2.5 fusion.2
  174.1 2.5 fusion.1
  179.6 18.6 %collective-permute-done.38 = bf16[2,2,2,96,768]{4,3,1,2,0:T(8,128)(2,1)S(1)} collective-permute-done((bf16[2,2,2,96,768]{4,3,1,2,0:T(8,128)(2,1)S(1)}, bf16[2,2,2,96,768]{4,3,1,2,0:T(8,128)(2,1)S(1)}, u32[]{:S(2)}, u32[]{:S(2)}) %collective-permute-start.38) | collective-permute-done | bytes 1179680 | tf_op jit(solution)/shard_map/ppermute | solution.py:37
  203.4 20.1 %collective-permute-done.33 = bf16[2,2,2,96,768]{4,3,1,2,0:T(8,128)(2,1)S(1)} collective-permute-done((bf16[2,2,2,96,768]{4,3,1,2,0:T(8,128)(2,1)S(1)}, bf16[2,2,2,96,768]{4,3,1,2,0:T(8,128)(2,1)S(1)}, u32[]{:S(2)}, u32[]{:S(2)}) %collective-permute-start.33) | collective-permute-done | bytes 1179680 | tf_op jit(solution)/shard_map/ppermute | solution.py:37
  228.7 11.4 %collective-permute-done.39 = bf16[2,2,96,768]{3,2,0,1:T(8,128)(2,1)S(1)} collective-permute-done((bf16[2,2,96,768]{3,2,0,1:T(8,128)(2,1)S(1)}, bf16[2,2,96,768]{3,2,0,1:T(8,128)(2,1)S(1)}, u32[]{:S(2)}, u32[]{:S(2)}) %collective-permute-start.39) | collective-permute-done | bytes 589856 | tf_op jit(solution)/shard_map/ppermute | solution.py:37
  242.6 8.3 %collective-permute-done.40 = bf16[2,96,768]{2,1,0:T(8,128)(2,1)S(1)} collective-permute-done((bf16[2,96,768]{2,1,0:T(8,128)(2,1)S(1)}, bf16[2,96,768]{2,1,0:T(8,128)(2,1)S(1)}, u32[]{:S(2)}, u32[]{:S(2)}) %collective-permute-start.40) | collective-permute-done | bytes 294944 | tf_op jit(solution)/shard_map/ppermute | solution.py:37
  251.1 4.5 %collective-permute-done.30 = bf16[2,96,768]{2,1,0:T(8,128)(2,1)S(1)} collective-permute-done((bf16[2,96,768]{2,1,0:T(8,128)(2,1)S(1)}, bf16[2,96,768]{2,1,0:T(8,128)(2,1)S(1)}, u32[]{:S(2)}, u32[]{:S(2)}) %collective-permute-start.30) | collective-permute-done | bytes 294944 | tf_op jit(solution)/shard_map/ppermute | solution.py:37
  256.0 2.5 collective-permute-start.35
  261.9 7.7 %collective-permute-done.35 = bf16[2,96,768]{2,1,0:T(8,128)(2,1)S(1)} collective-permute-done((bf16[2,96,768]{2,1,0:T(8,128)(2,1)S(1)}, bf16[2,96,768]{2,1,0:T(8,128)(2,1)S(1)}, u32[]{:S(2)}, u32[]{:S(2)}) %collective-permute-start.35) | collective-permute-done | bytes 294944 | tf_op jit(solution)/shard_map/ppermute | solution.py:37
  270.4 3.0 %collective-permute-done.25 = bf16[2,96,768]{2,1,0:T(8,128)(2,1)S(1)} collective-permute-done((bf16[2,96,768]{2,1,0:T(8,128)(2,1)S(1)}, bf16[2,96,768]{2,1,0:T(8,128)(2,1)S(1)}, u32[]{:S(2)}, u32[]{:S(2)}) %collective-permute-start.25) | collective-permute-done | bytes 294944 | tf_op jit(solution)/shard_map/ppermute | solution.py:37
  274.2 4.9 %collective-permute-done.36 = bf16[96,768]{1,0:T(8,128)(2,1)S(1)} collective-permute-done((bf16[96,768]{1,0:T(8,128)(2,1)S(1)}, bf16[96,768]{1,0:T(8,128)(2,1)S(1)}, u32[]{:S(2)}, u32[]{:S(2)}) %collective-permute-start.36) | collective-permute-done | bytes 147488 | tf_op jit(solution)/shard_map/ppermute | solution.py:37
  280.0 2.3 collective-permute-done.26
  (268 shorter events, 97.9 us)
Async XLA Ops:
  0.6 13.2 %collective-permute-start = (bf16[256,768]{1,0:T(8,128)(2,1)}, bf16[256,768]{1,0:T(8,128)(2,1)S(1)}, u32[]{:S(2)}, u32[]{:S(2)}) collective-permute-start(bf16[256,768]{1,0:T(8,128)(2,1)} %bitcast.230), channel_id=1, source_target_pairs={{0,8},{8,0},{16,24},{24,16},{1,9},{9,1},{17,25},{25,17},{2,10},{10... | collective-permute-start | bytes 1179656 | tf_op jit(solution)/shard_map/ppermute | solution.py:37
  3.6 19.2 %collective-permute-start.1 = (bf16[256,768]{1,0:T(8,128)(2,1)}, bf16[256,768]{1,0:T(8,128)(2,1)S(1)}, u32[]{:S(2)}, u32[]{:S(2)}) collective-permute-start(bf16[256,768]{1,0:T(8,128)(2,1)} %bitcast.231), channel_id=1, source_target_pairs={{0,16},{8,24},{16,0},{24,8},{1,17},{9,25},{17,1},{25,9},{2,18},{10... | collective-permute-start | bytes 1179656 | tf_op jit(solution)/shard_map/ppermute | solution.py:37
  5.2 17.7 %collective-permute-start.2 = (bf16[256,768]{1,0:T(8,128)(2,1)}, bf16[256,768]{1,0:T(8,128)(2,1)S(1)}, u32[]{:S(2)}, u32[]{:S(2)}) collective-permute-start(bf16[256,768]{1,0:T(8,128)(2,1)} %bitcast.232), channel_id=1, source_target_pairs={{0,24},{8,16},{16,8},{24,0},{1,25},{9,17},{17,9},{25,1},{2,26},{10... | collective-permute-start | bytes 1179656 | tf_op jit(solution)/shard_map/ppermute | solution.py:37
  35.3 12.2 %collective-permute-start.3 = (bf16[256,768]{1,0:T(8,128)(2,1)S(1)}, bf16[256,768]{1,0:T(8,128)(2,1)}, u32[]{:S(2)}, u32[]{:S(2)}) collective-permute-start(bf16[256,768]{1,0:T(8,128)(2,1)S(1)} %fusion.127), channel_id=1, source_target_pairs={{0,8},{8,0},{16,24},{24,16},{1,9},{9,1},{17,25},{25,17},{2,10},{10... | collective-permute-start | bytes 1179656 | tf_op jit(solution)/shard_map/ppermute | solution.py:37
  36.6 18.2 %collective-permute-start.4 = (bf16[256,768]{1,0:T(8,128)(2,1)S(1)}, bf16[256,768]{1,0:T(8,128)(2,1)}, u32[]{:S(2)}, u32[]{:S(2)}) collective-permute-start(bf16[256,768]{1,0:T(8,128)(2,1)S(1)} %fusion.127), channel_id=1, source_target_pairs={{0,16},{8,24},{16,0},{24,8},{1,17},{9,25},{17,1},{25,9},{2,18},{10... | collective-permute-start | bytes 1179656 | tf_op jit(solution)/shard_map/ppermute | solution.py:37
  37.4 17.4 %collective-permute-start.5 = (bf16[256,768]{1,0:T(8,128)(2,1)S(1)}, bf16[256,768]{1,0:T(8,128)(2,1)}, u32[]{:S(2)}, u32[]{:S(2)}) collective-permute-start(bf16[256,768]{1,0:T(8,128)(2,1)S(1)} %fusion.127), channel_id=1, source_target_pairs={{0,24},{8,16},{16,8},{24,0},{1,25},{9,17},{17,9},{25,1},{2,26},{10... | collective-permute-start | bytes 1179656 | tf_op jit(solution)/shard_map/ppermute | solution.py:37
  72.2 24.6 %collective-permute-start.6 = (bf16[256,768]{1,0:T(8,128)(2,1)S(1)}, bf16[256,768]{1,0:T(8,128)(2,1)S(1)}, u32[]{:S(2)}, u32[]{:S(2)}) collective-permute-start(bf16[256,768]{1,0:T(8,128)(2,1)S(1)} %get-tuple-element.39), channel_id=1, source_target_pairs={{0,8},{8,0},{16,24},{24,16},{1,9},{9,1},{17,25},{25,17},{2,10},{10... | collective-permute-start | bytes 1179656 | tf_op jit(solution)/shard_map/ppermute | solution.py:37
  72.9 24.0 %collective-permute-start.7 = (bf16[256,768]{1,0:T(8,128)(2,1)S(1)}, bf16[256,768]{1,0:T(8,128)(2,1)S(1)}, u32[]{:S(2)}, u32[]{:S(2)}) collective-permute-start(bf16[256,768]{1,0:T(8,128)(2,1)S(1)} %get-tuple-element.39), channel_id=1, source_target_pairs={{0,16},{8,24},{16,0},{24,8},{1,17},{9,25},{17,1},{25,9},{2,18},{10... | collective-permute-start | bytes 1179656 | tf_op jit(solution)/shard_map/ppermute | solution.py:37
  74.0 22.8 %collective-permute-start.8 = (bf16[256,768]{1,0:T(8,128)(2,1)S(1)}, bf16[256,768]{1,0:T(8,128)(2,1)S(1)}, u32[]{:S(2)}, u32[]{:S(2)}) collective-permute-start(bf16[256,768]{1,0:T(8,128)(2,1)S(1)} %get-tuple-element.39), channel_id=1, source_target_pairs={{0,24},{8,16},{16,8},{24,0},{1,25},{9,17},{17,9},{25,1},{2,26},{10... | collective-permute-start | bytes 1179656 | tf_op jit(solution)/shard_map/ppermute | solution.py:37
  88.4 78.2 %collective-permute-start.37 = (bf16[2,2,2,2,96,768]{5,4,2,3,0,1:T(8,128)(2,1)}, bf16[2,2,2,2,96,768]{5,4,2,3,0,1:T(8,128)(2,1)}, u32[]{:S(2)}, u32[]{:S(2)}) collective-permute-start(bf16[2,2,2,2,96,768]{5,4,2,3,0,1:T(8,128)(2,1)} %bitcast.221), channel_id=1, source_target_pairs={{0,1},{1,0},{2,3},{3,2},{4,5},{5,4},{6,7},{7,6},{8,9},{9,8},{10,11... | collective-permute-start | bytes 7077896 | tf_op jit(solution)/shard_map/ppermute | solution.py:37
  96.8 73.7 %collective-permute-start.27 = (bf16[2,2,2,2,96,768]{5,4,2,3,1,0:T(8,128)(2,1)}, bf16[2,2,2,2,96,768]{5,4,2,3,1,0:T(8,128)(2,1)}, u32[]{:S(2)}, u32[]{:S(2)}) collective-permute-start(bf16[2,2,2,2,96,768]{5,4,2,3,1,0:T(8,128)(2,1)} %bitcast.223), channel_id=1, source_target_pairs={{0,1},{1,0},{2,3},{3,2},{4,5},{5,4},{6,7},{7,6},{8,9},{9,8},{10,11... | collective-permute-start | bytes 7077896 | tf_op jit(solution)/shard_map/ppermute | solution.py:37
  130.0 20.5 %collective-permute-start.10 = (bf16[256,768]{1,0:T(8,128)(2,1)}, bf16[256,768]{1,0:T(8,128)(2,1)}, u32[]{:S(2)}, u32[]{:S(2)}) collective-permute-start(bf16[256,768]{1,0:T(8,128)(2,1)} %get-tuple-element.37), channel_id=1, source_target_pairs={{0,16},{8,24},{16,0},{24,8},{1,17},{9,25},{17,1},{25,9},{2,18},{10... | collective-permute-start | bytes 1179656 | tf_op jit(solution)/shard_map/ppermute | solution.py:37
  131.4 21.5 %collective-permute-start.11 = (bf16[256,768]{1,0:T(8,128)(2,1)}, bf16[256,768]{1,0:T(8,128)(2,1)}, u32[]{:S(2)}, u32[]{:S(2)}) collective-permute-start(bf16[256,768]{1,0:T(8,128)(2,1)} %get-tuple-element.37), channel_id=1, source_target_pairs={{0,24},{8,16},{16,8},{24,0},{1,25},{9,17},{17,9},{25,1},{2,26},{10... | collective-permute-start | bytes 1179656 | tf_op jit(solution)/shard_map/ppermute | solution.py:37
  132.7 9.3 %collective-permute-start.15 = (f32[6912]{0:T(1024)S(1)}, f32[6912]{0:T(1024)S(1)}, u32[]{:S(2)}, u32[]{:S(2)}) collective-permute-start(f32[6912]{0:T(1024)S(1)} %add.372), channel_id=1, source_target_pairs={{0,8},{8,0},{16,24},{24,16},{1,9},{9,1},{17,25},{25,17},{2,10},{10... | collective-permute-start | bytes 82952 | tf_op jit(solution)/shard_map/ppermute | solution.py:37
  149.2 24.9 %collective-permute-start.32 = (bf16[2,2,2,2,96,768]{5,4,2,3,0,1:T(8,128)(2,1)}, bf16[2,2,2,2,96,768]{5,4,2,3,0,1:T(8,128)(2,1)}, u32[]{:S(2)}, u32[]{:S(2)}) collective-permute-start(bf16[2,2,2,2,96,768]{5,4,2,3,0,1:T(8,128)(2,1)} %bitcast.222), channel_id=1, source_target_pairs={{0,1},{1,0},{2,3},{3,2},{4,5},{5,4},{6,7},{7,6},{8,9},{9,8},{10,11... | collective-permute-start | bytes 7077896 | tf_op jit(solution)/shard_map/ppermute | solution.py:37
  150.5 11.7 %collective-permute-start.9 = (bf16[256,768]{1,0:T(8,128)(2,1)}, bf16[256,768]{1,0:T(8,128)(2,1)S(1)}, u32[]{:S(2)}, u32[]{:S(2)}) collective-permute-start(bf16[256,768]{1,0:T(8,128)(2,1)} %get-tuple-element.37), channel_id=1, source_target_pairs={{0,8},{8,0},{16,24},{24,16},{1,9},{9,1},{17,25},{25,17},{2,10},{10... | collective-permute-start | bytes 1179656 | tf_op jit(solution)/shard_map/ppermute | solution.py:37
  152.9 25.2 %collective-permute-start.22 = (bf16[2,2,2,2,96,768]{5,4,2,3,1,0:T(8,128)(2,1)}, bf16[2,2,2,2,96,768]{5,4,2,3,1,0:T(8,128)(2,1)S(1)}, u32[]{:S(2)}, u32[]{:S(2)}) collective-permute-start(bf16[2,2,2,2,96,768]{5,4,2,3,1,0:T(8,128)(2,1)} %bitcast.229), channel_id=1, source_target_pairs={{0,1},{1,0},{2,3},{3,2},{4,5},{5,4},{6,7},{7,6},{8,9},{9,8},{10,11... | collective-permute-start | bytes 7077896 | tf_op jit(solution)/shard_map/ppermute | solution.py:37
  169.3 28.9 %collective-permute-start.38 = (bf16[2,2,2,96,768]{4,3,1,2,0:T(8,128)(2,1)S(1)}, bf16[2,2,2,96,768]{4,3,1,2,0:T(8,128)(2,1)S(1)}, u32[]{:S(2)}, u32[]{:S(2)}) collective-permute-start(bf16[2,2,2,96,768]{4,3,1,2,0:T(8,128)(2,1)S(1)} %dynamic-slice_bitcast_fusion), channel_id=1, source_target_pairs={{0,8},{8,0},{16,24},{24,16},{1,9},{9,1},{17,25},{25,17},{2,10},{10... | collective-permute-start | bytes 3538952 | tf_op jit(solution)/shard_map/ppermute | solution.py:37
  173.1 29.0 %collective-permute-start.28 = (bf16[2,2,2,96,768]{4,3,1,2,0:T(8,128)(2,1)S(1)}, bf16[2,2,2,96,768]{4,3,1,2,0:T(8,128)(2,1)S(1)}, u32[]{:S(2)}, u32[]{:S(2)}) collective-permute-start(bf16[2,2,2,96,768]{4,3,1,2,0:T(8,128)(2,1)S(1)} %dynamic-slice_bitcast_fusion.2), channel_id=1, source_target_pairs={{0,16},{8,24},{16,0},{24,8},{1,17},{9,25},{17,1},{25,9},{2,18},{10... | collective-permute-start | bytes 3538952 | tf_op jit(solution)/shard_map/ppermute | solution.py:37
  176.7 46.8 %collective-permute-start.33 = (bf16[2,2,2,96,768]{4,3,1,2,0:T(8,128)(2,1)S(1)}, bf16[2,2,2,96,768]{4,3,1,2,0:T(8,128)(2,1)S(1)}, u32[]{:S(2)}, u32[]{:S(2)}) collective-permute-start(bf16[2,2,2,96,768]{4,3,1,2,0:T(8,128)(2,1)S(1)} %dynamic-slice_bitcast_fusion.1), channel_id=1, source_target_pairs={{0,8},{8,0},{16,24},{24,16},{1,9},{9,1},{17,25},{25,17},{2,10},{10... | collective-permute-start | bytes 3538952 | tf_op jit(solution)/shard_map/ppermute | solution.py:37
  178.9 48.4 %collective-permute-start.23 = (bf16[2,2,2,96,768]{4,3,1,2,0:T(8,128)(2,1)S(1)}, bf16[2,2,2,96,768]{4,3,1,2,0:T(8,128)(2,1)S(1)}, u32[]{:S(2)}, u32[]{:S(2)}) collective-permute-start(bf16[2,2,2,96,768]{4,3,1,2,0:T(8,128)(2,1)S(1)} %dynamic-slice_bitcast_fusion.3), channel_id=1, source_target_pairs={{0,16},{8,24},{16,0},{24,8},{1,17},{9,25},{17,1},{25,9},{2,18},{10... | collective-permute-start | bytes 3538952 | tf_op jit(solution)/shard_map/ppermute | solution.py:37
  198.6 41.5 %collective-permute-start.39 = (bf16[2,2,96,768]{3,2,0,1:T(8,128)(2,1)S(1)}, bf16[2,2,96,768]{3,2,0,1:T(8,128)(2,1)S(1)}, u32[]{:S(2)}, u32[]{:S(2)}) collective-permute-start(bf16[2,2,96,768]{3,2,0,1:T(8,128)(2,1)S(1)} %dynamic-slice_bitcast_fusion.4), channel_id=1, source_target_pairs={{0,16},{8,24},{16,0},{24,8},{1,17},{9,25},{17,1},{25,9},{2,18},{10... | collective-permute-start | bytes 1769480 | tf_op jit(solution)/shard_map/ppermute | solution.py:37
  202.5 39.4 %collective-permute-start.29 = (bf16[2,2,96,768]{3,2,0,1:T(8,128)(2,1)S(1)}, bf16[2,2,96,768]{3,2,0,1:T(8,128)(2,1)S(1)}, u32[]{:S(2)}, u32[]{:S(2)}) collective-permute-start(bf16[2,2,96,768]{3,2,0,1:T(8,128)(2,1)S(1)} %dynamic-slice_bitcast_fusion.6), channel_id=1, source_target_pairs={{0,8},{8,0},{16,24},{24,16},{1,9},{9,1},{17,25},{25,17},{2,10},{10... | collective-permute-start | bytes 1769480 | tf_op jit(solution)/shard_map/ppermute | solution.py:37
  223.8 31.9 %collective-permute-start.34 = (bf16[2,2,96,768]{3,2,0,1:T(8,128)(2,1)S(1)}, bf16[2,2,96,768]{3,2,0,1:T(8,128)(2,1)S(1)}, u32[]{:S(2)}, u32[]{:S(2)}) collective-permute-start(bf16[2,2,96,768]{3,2,0,1:T(8,128)(2,1)S(1)} %dynamic-slice_bitcast_fusion.5), channel_id=1, source_target_pairs={{0,16},{8,24},{16,0},{24,8},{1,17},{9,25},{17,1},{25,9},{2,18},{10... | collective-permute-start | bytes 1769480 | tf_op jit(solution)/shard_map/ppermute | solution.py:37
  227.8 30.7 %collective-permute-start.24 = (bf16[2,2,96,768]{3,2,0,1:T(8,128)(2,1)S(1)}, bf16[2,2,96,768]{3,2,0,1:T(8,128)(2,1)S(1)}, u32[]{:S(2)}, u32[]{:S(2)}) collective-permute-start(bf16[2,2,96,768]{3,2,0,1:T(8,128)(2,1)S(1)} %dynamic-slice_bitcast_fusion.7), channel_id=1, source_target_pairs={{0,8},{8,0},{16,24},{24,16},{1,9},{9,1},{17,25},{25,17},{2,10},{10... | collective-permute-start | bytes 1769480 | tf_op jit(solution)/shard_map/ppermute | solution.py:37
  240.2 10.6 %collective-permute-start.40 = (bf16[2,96,768]{2,1,0:T(8,128)(2,1)S(1)}, bf16[2,96,768]{2,1,0:T(8,128)(2,1)S(1)}, u32[]{:S(2)}, u32[]{:S(2)}) collective-permute-start(bf16[2,96,768]{2,1,0:T(8,128)(2,1)S(1)} %dynamic-slice_bitcast_fusion.8), channel_id=1, source_target_pairs={{0,2},{1,3},{2,0},{3,1},{4,6},{5,7},{6,4},{7,5},{8,10},{9,11},{10,... | collective-permute-start | bytes 884744 | tf_op jit(solution)/shard_map/ppermute | solution.py:37
  242.1 13.5 %collective-permute-start.30 = (bf16[2,96,768]{2,1,0:T(8,128)(2,1)S(1)}, bf16[2,96,768]{2,1,0:T(8,128)(2,1)S(1)}, u32[]{:S(2)}, u32[]{:S(2)}) collective-permute-start(bf16[2,96,768]{2,1,0:T(8,128)(2,1)S(1)} %dynamic-slice_bitcast_fusion.10), channel_id=1, source_target_pairs={{0,2},{1,3},{2,0},{3,1},{4,6},{5,7},{6,4},{7,5},{8,10},{9,11},{10,... | collective-permute-start | bytes 884744 | tf_op jit(solution)/shard_map/ppermute | solution.py:37
  251.0 8.8 %collective-permute-start.41 = (bf16[96,768]{1,0:T(8,128)(2,1)S(1)}, bf16[96,768]{1,0:T(8,128)(2,1)S(1)}, u32[]{:S(2)}, u32[]{:S(2)}) collective-permute-start(bf16[96,768]{1,0:T(8,128)(2,1)S(1)} %dynamic-slice_bitcast_fusion.12), channel_id=1, source_target_pairs={{0,4},{1,5},{2,6},{3,7},{4,0},{5,1},{6,2},{7,3},{8,12},{9,13},{10,... | collective-permute-start | bytes 442376 | tf_op jit(solution)/shard_map/ppermute | solution.py:37
  256.0 13.6 %collective-permute-start.35 = (bf16[2,96,768]{2,1,0:T(8,128)(2,1)S(1)}, bf16[2,96,768]{2,1,0:T(8,128)(2,1)S(1)}, u32[]{:S(2)}, u32[]{:S(2)}) collective-permute-start(bf16[2,96,768]{2,1,0:T(8,128)(2,1)S(1)} %dynamic-slice_bitcast_fusion.9), channel_id=1, source_target_pairs={{0,2},{1,3},{2,0},{3,1},{4,6},{5,7},{6,4},{7,5},{8,10},{9,11},{10,... | collective-permute-start | bytes 884744 | tf_op jit(solution)/shard_map/ppermute | solution.py:37
  258.7 14.6 %collective-permute-start.25 = (bf16[2,96,768]{2,1,0:T(8,128)(2,1)S(1)}, bf16[2,96,768]{2,1,0:T(8,128)(2,1)S(1)}, u32[]{:S(2)}, u32[]{:S(2)}) collective-permute-start(bf16[2,96,768]{2,1,0:T(8,128)(2,1)S(1)} %dynamic-slice_bitcast_fusion.11), channel_id=1, source_target_pairs={{0,2},{1,3},{2,0},{3,1},{4,6},{5,7},{6,4},{7,5},{8,10},{9,11},{10,... | collective-permute-start | bytes 884744 | tf_op jit(solution)/shard_map/ppermute | solution.py:37
  269.7 9.4 %collective-permute-start.36 = (bf16[96,768]{1,0:T(8,128)(2,1)S(1)}, bf16[96,768]{1,0:T(8,128)(2,1)S(1)}, u32[]{:S(2)}, u32[]{:S(2)}) collective-permute-start(bf16[96,768]{1,0:T(8,128)(2,1)S(1)} %dynamic-slice_bitcast_fusion.13), channel_id=1, source_target_pairs={{0,4},{1,5},{2,6},{3,7},{4,0},{5,1},{6,2},{7,3},{8,12},{9,13},{10,... | collective-permute-start | bytes 442376 | tf_op jit(solution)/shard_map/ppermute | solution.py:37
  273.4 8.9 %collective-permute-start.26 = (bf16[96,768]{1,0:T(8,128)(2,1)S(1)}, bf16[96,768]{1,0:T(8,128)(2,1)S(1)}, u32[]{:S(2)}, u32[]{:S(2)}) collective-permute-start(bf16[96,768]{1,0:T(8,128)(2,1)S(1)} %dynamic-slice_bitcast_fusion.15), channel_id=1, source_target_pairs={{0,4},{1,5},{2,6},{3,7},{4,0},{5,1},{6,2},{7,3},{8,12},{9,13},{10,... | collective-permute-start | bytes 442376 | tf_op jit(solution)/shard_map/ppermute | solution.py:37
  (51 other events, 377.3 us)
